TPU v7x, 128 devices: a whole 4x4x4 slice. The times are simulated.
128 devices in a mesh: group: 8 (over z, x_hi), head: 16 (over x_lo, y, core).
Axes of the slice: x: 4 (x_hi: 2, x_lo: 2; x = x_hi * 2 + x_lo), y: 4, z: 4, core: 2. Of those that a mesh axis runs over, the one named last changes fastest.
Arguments:
- states: float32 [256, 32, 128, 128], P('group', 'head'), may hold values from -6 to 6
- placement: int32 [256, 1], replicated, may hold values from 0 to 31; in each aligned block of 32 rows (0 to 31, 32 to 63, ...) at most 2 rows name the same one
- queries: bfloat16 [8, 16, 8, 2, 8, 512], P('group', 'head'), may hold values from -6 to 6
- key_vectors: bfloat16 [8, 16, 8, 2, 8, 512], P('group', 'head'), may hold values from -6 to 6
- value_vectors: bfloat16 [8, 16, 8, 2, 8, 1024], P('group', 'head'), may hold values from -6 to 6
- gate_inputs: bfloat16 [8, 16, 8, 2, 8, 1024], P('group', 'head'), may hold values from -6 to 6
- write_strength: float32 [8, 16, 8, 2, 8, 8], P('group', 'head'), may hold values from 0.05 to 1
- decay_rate: float32 [8, 16, 8, 2, 8, 8], P('group', 'head'), may hold values from 0.02 to 1
- norm_gain: float32 [128], replicated, may hold values from 0.25 to 1.75
Outputs:
- decoded: bfloat16 [8, 16, 8, 2, 8, 1024], P('group', 'head')
- final_states: float32 [8, 16, 8, 2, 8, 128, 128], P('group', 'head')
Inputs may be any that keep to these rules, and one draw needn't show every extreme that they name: `placement`: among the requests of one prefill group no decode group is named more than 2 times, and some decode group exactly 2 times.
All inputs are finite; a program needn't handle non-finite values.
Results may differ from a plain program's by a relative error of at most 0.001.
Values sent between devices are 32-bit elements; how exact they have to be, the bound alone decides.
No kernel may reach another device: no remote copies, remote signals or barrier semaphores. Data moves between devices by JAX's collectives and lax.ppermute only.
A program may use at most 128 MiB of HBM per device.

v0:
```python
import math

import jax
import jax.numpy as jnp
from jax import lax
from jax.experimental import pallas as pl
from jax.experimental.pallas import tpu as pltpu
from jax.sharding import Mesh
from jax.sharding import PartitionSpec as P

SUBGROUPS = 4
SLOT_CAP = 2
CORES = 2
SOURCES = 2
EPS = 1e-06


def fits_kernel(dec_groups, reqs, placed, fits):
    lanes = placed.shape[1]
    chips = placed[...] // CORES
    named = [jnp.where(chips == chip, 1.0, 0.0) for chip in range(dec_groups // CORES)]
    lane = lax.broadcasted_iota(jnp.int32, (lanes, lanes), 0)
    group = lax.broadcasted_iota(jnp.int32, (lanes, lanes), 1)
    counts = jnp.dot(
        jnp.concatenate(named, axis=0).astype(jnp.bfloat16),
        jnp.where(lane // reqs == group, 1.0, 0.0).astype(jnp.bfloat16),
        preferred_element_type=jnp.float32,
    )
    fits[0] = jnp.where(jnp.max(counts) < SLOT_CAP + 1.5, 1, 0)


def cells_fit(placed, dec_groups, reqs):
    return pl.pallas_call(
        lambda *refs: fits_kernel(dec_groups, reqs, *refs),
        out_shape=jax.ShapeDtypeStruct((1,), jnp.int32),
        in_specs=[pl.BlockSpec(memory_space=pltpu.VMEM)],
        out_specs=pl.BlockSpec(memory_space=pltpu.SMEM),
    )(placed.reshape(-1, 128))


def pack_kernel(n_group, reqs, spare, placed, states, cells, live, count, sems):
    group = lax.axis_index("group")
    mine = group * SUBGROUPS + lax.axis_index("sub")
    heads = states.shape[1]

    def clear(d, carry):
        count[d] = 0
        return carry

    lax.fori_loop(0, n_group * SUBGROUPS, clear, 0, unroll=8)

    def send(r, carry):
        d = placed[group * reqs + r]
        rank = count[d]
        count[d] = rank + 1
        if spare:

            @pl.when(rank == 0)
            def _():
                pltpu.make_async_copy(
                    states.at[r], cells.at[d, pl.ds(0, heads)], sems.at[r]
                ).start()

            @pl.when(rank > 0)
            def _():
                for a in range(heads):
                    pltpu.make_async_copy(
                        states.at[r, a], cells.at[d // CORES * CORES + a, heads], sems.at[r]
                    ).start()

        else:
            pltpu.make_async_copy(states.at[r], cells.at[d, rank], sems.at[r]).start()
        return carry

    lax.fori_loop(0, reqs, send, 0, unroll=4)

    for s in range(n_group):

        def tally(r, total, s=s):
            return total + jnp.where(placed[s * reqs + r] == mine, 1, 0)

        live[s] = lax.fori_loop(0, reqs, tally, 0, unroll=8)

    def drain(r, carry):
        landed = cells.at[0, pl.ds(0, heads)] if spare else cells.at[0, 0]
        pltpu.make_async_copy(states.at[r], landed, sems.at[r]).wait()
        return carry

    lax.fori_loop(0, reqs, drain, 0, unroll=4)


def pack(placed, states, n_group, spare):
    reqs, heads, key_size, value_size = states.shape
    cell = (heads + 1,) if spare else (SLOT_CAP, heads)
    cells = (n_group * SUBGROUPS,) + cell + (key_size, value_size)
    return pl.pallas_call(
        lambda *refs: pack_kernel(n_group, reqs, spare, *refs),
        out_shape=(
            pltpu.VMEM(cells, states.dtype),
            jax.ShapeDtypeStruct((n_group,), jnp.int32),
        ),
        in_specs=[
            pl.BlockSpec(memory_space=pltpu.SMEM),
            pl.BlockSpec(memory_space=pltpu.HBM),
        ],
        out_specs=(
            pl.BlockSpec(memory_space=pltpu.VMEM),
            pl.BlockSpec(memory_space=pltpu.SMEM),
        ),
        scratch_shapes=[
            pltpu.SMEM((n_group * SUBGROUPS,), jnp.int32),
            pltpu.SemaphoreType.DMA((reqs,)),
        ],
        compiler_params=pltpu.CompilerParams(vmem_limit_bytes=32 * 1024 * 1024),
    )(placed, pltpu.with_memory_space_constraint(states, pltpu.HBM))


def split(x):
    high = x.astype(jnp.bfloat16)
    return high, (x - high.astype(jnp.float32)).astype(jnp.bfloat16)


def row_sums(parts):
    rows, lanes = parts[0].shape
    high, low = split(jnp.concatenate(parts, axis=0))
    sums = jnp.dot(
        jnp.concatenate([high, low], axis=1),
        jnp.ones((2 * lanes, lanes), jnp.bfloat16),
        preferred_element_type=jnp.float32,
    )
    return [sums[n * rows : (n + 1) * rows] for n in range(len(parts))]


def widen(columns, width):
    rows, count = columns.shape
    high, rest = split(columns)
    low = columns - high.astype(jnp.float32) - rest.astype(jnp.float32)
    parts = [high.astype(jnp.float32), rest.astype(jnp.float32), low]
    lane = lax.broadcasted_iota(jnp.int32, (count, count * width), 1)
    column = lax.broadcasted_iota(jnp.int32, (count, count * width), 0)
    wide = jnp.dot(
        jnp.concatenate(parts, axis=0).astype(jnp.bfloat16),
        jnp.where(lane // width == column, 1.0, 0.0).astype(jnp.bfloat16),
        preferred_element_type=jnp.float32,
    )
    return wide[:rows] + wide[rows : 2 * rows] + wide[2 * rows :]


def decode_kernel(
    load, chosen, slot, first, live, query, key, value, gate, strength, decay, gain, tokens, states,
    by_key, by_query, values, fades, writes, key_rows, query_rows, kept,
):
    size, width = states.shape[2:]
    heads = states.shape[1] // SUBGROUPS
    steps = key.shape[4]
    units = [(n, i) for n in range(SOURCES) for i in range(SUBGROUPS)]
    count = len(units)

    def keys(i):
        return slice(i * size, (i + 1) * size)

    def lanes(i):
        return slice(i * heads * width, (i + 1) * heads * width)

    def state_of(n, i):
        return jnp.concatenate(
            [states[first + n, heads * i + a] for a in range(heads)]
            if chosen
            else load(first + n, i),
            axis=1,
        )

    def rows(t):
        return slice(t * count, (t + 1) * count)

    def spread(ref, u, x):
        for a in range(heads):
            ref[a, pl.ds(u, steps, stride=count), :] = x[:, a * width : (a + 1) * width]

    def gather(ref, u):
        return jnp.concatenate(
            [ref[a, pl.ds(u, steps, stride=count), :] for a in range(heads)], axis=1
        )

    wide = widen(
        jnp.concatenate(
            [x[0, 0, first + n, slot] for x in (decay, strength) for n in range(SOURCES)], axis=0
        ),
        width,
    )
    for u, (n, i) in enumerate(units):
        key_f = key[0, 0, first + n, slot, :, keys(i)].astype(jnp.float32)
        query_f = query[0, 0, first + n, slot, :, keys(i)].astype(jnp.float32)
        both = jnp.concatenate([key_f, query_f], axis=0).astype(jnp.bfloat16)
        before = load(first + n, i)
        if chosen:
            for a in range(heads):
                states[first + n, heads * i + a] = before[a]
        high, low = split(jnp.concatenate(before, axis=1))
        product = jnp.dot(
            jnp.concatenate([both, both], axis=1),
            jnp.concatenate([high, low], axis=0),
            preferred_element_type=jnp.float32,
        )
        spread(by_key, u, product[:steps])
        spread(by_query, u, product[steps:])
        key_rows[pl.ds(u, steps, stride=count), :] = key_f
        query_rows[pl.ds(u, steps, stride=count), :] = query_f
        spread(values, u, value[0, 0, first + n, slot, :, lanes(i)].astype(jnp.float32))
        spread(fades, u, wide[n * steps : (n + 1) * steps, lanes(i)])
        spread(writes, u, wide[(SOURCES + n) * steps : (SOURCES + n + 1) * steps, lanes(i)])

    on_key = [[by_key[a, rows(t)] for a in range(heads)] for t in range(steps)]
    on_query = [[by_query[a, rows(t)] for a in range(heads)] for t in range(steps)]
    keyed = [key_rows[rows(t)] for t in range(steps)]
    asked = [query_rows[rows(t)] for t in range(steps)]
    pairs = [(l, t) for t in range(steps) for l in range(t, steps)]
    key_key = dict(zip(pairs, row_sums([keyed[l] * keyed[t] for l, t in pairs])))
    query_key = dict(zip(pairs, row_sums([asked[l] * keyed[t] for l, t in pairs])))
    query_norms = [lax.rsqrt(x + EPS) / math.sqrt(size) for x in row_sums([q * q for q in asked])]
    written, total = [], None
    for t in range(steps):
        fade = [fades[a, rows(t)] for a in range(heads)]
        total = fade if total is None else [x * f for x, f in zip(total, fade)]
        norm = lax.rsqrt(key_key[t, t] + EPS)
        write = []
        for a in range(heads):
            residual = values[a, rows(t)] - norm * (on_key[t][a] * fade[a])
            write.append(writes[a, rows(t)] * norm * residual)
        written = [[w * f for w, f in zip(old, fade)] for old in written] + [write]
        for later in range(t, steps):
            for on, dots in ((on_key, key_key), (on_query, query_key)):
                if on is on_query or later > t:
                    dot = dots[later, t]
                    on[later] = [x * f + dot * w for x, f, w in zip(on[later], fade, write)]
    kept[...] = jnp.concatenate(total, axis=1)
    readouts = [x * query_norms[t] for t in range(steps) for x in on_query[t]]
    squares = row_sums([x * x for x in readouts])
    for t in range(steps):
        for a in range(heads):
            by_key[a, rows(t)] = written[t][a]
            norm = lax.rsqrt(squares[t * heads + a] / width + EPS)
            by_query[a, rows(t)] = readouts[t * heads + a] * norm * gain[...]

    for u, (n, i) in enumerate(units):
        key_f = key[0, 0, first + n, slot, :, keys(i)].astype(jnp.float32)
        high, low = split(gather(by_key, u))
        update = lax.dot_general(
            jnp.concatenate([key_f, key_f], axis=0).astype(jnp.bfloat16),
            jnp.concatenate([high.astype(jnp.float32), low.astype(jnp.float32)], axis=0).astype(
                jnp.bfloat16
            ),
            (((0,), (0,)), ((), ())),
            preferred_element_type=jnp.float32,
        )
        state = kept[u : u + 1, :] * state_of(n, i) + update
        for a in range(heads):
            states[first + n, heads * i + a] = state[:, a * width : (a + 1) * width]
        opened = gate[0, 0, first + n, slot, :, lanes(i)].astype(jnp.float32)
        token = gather(by_query, u) * (opened * jax.nn.sigmoid(opened))
        tokens[first + n, :, lanes(i)] = token.astype(tokens.dtype)

    for n in range(SOURCES):

        @pl.when(live[first + n] <= slot)
        def _(n=n):
            tokens[first + n] = jnp.zeros(tokens.shape[1:], tokens.dtype)
            states[first + n] = jnp.zeros(states.shape[1:], states.dtype)


def decode(live, sources, load, slot, small, gain, earlier=None):
    queries, values = small[0], small[2]
    n_group, cap, steps = queries.shape[2:5]
    key_size, value_size = queries.shape[5] // SUBGROUPS, gain.shape[1]
    heads = values.shape[5] // (SUBGROUPS * value_size)
    block = (SUBGROUPS * heads, key_size, value_size)
    units = SOURCES * SUBGROUPS
    rows = steps * units
    by_step = (heads, rows, value_size)
    scratch = [by_step] * 5 + [(rows, key_size)] * 2 + [(units, heads * value_size)]
    kept = () if earlier is None else earlier

    def kernel(live, *refs):
        blocks, refs = refs[: len(sources)], refs[len(sources) :]
        ins, refs = refs[: len(small) + 1], refs[len(small) + 1 :]
        before, refs = refs[: len(kept)], refs[len(kept) :]
        result, finals, states, sems, *work = refs
        tokens, blank = work.pop(), work.pop()
        n_sem = 2 * n_group

        def erase(group):
            return pltpu.make_async_copy(
                blank, finals.at[0, 0, group, cap - 1], sems.at[n_group + group]
            )

        def place(group):
            return pltpu.make_async_copy(
                states.at[group], finals.at[0, 0, group, slot], sems.at[group]
            )

        def run(batch, carry):
            first = batch * SOURCES

            def compute():
                decode_kernel(
                    lambda s, i: load(s, i, *blocks), len(sources) > 1, slot, first, live, *ins,
                    tokens.at[0, 0, :, slot], states, *work,
                )

            if kept:
                some = live[first] > slot
                for n in range(1, SOURCES):
                    some = some | (live[first + n] > slot)
                pl.when(some)(compute)
                for n in range(SOURCES):
                    pl.when(live[first + n] > slot)(lambda n=n: place(first + n).start())
            else:
                compute()
                for n in range(SOURCES):
                    place(first + n).start()
            return carry

        def add_slot():
            copy = pltpu.make_async_copy(result, tokens, sems.at[n_sem])
            copy.start()
            copy.wait()
            lax.fori_loop(0, n_group // SOURCES, run, 0)
            copy = pltpu.make_async_copy(tokens, result, sems.at[n_sem])
            copy.start()
            for group in range(n_group):
                pl.when(live[group] > slot)(lambda group=group: place(group).wait())
            copy.wait()

        if kept:
            some = live[0] > slot
            for group in range(1, n_group):
                some = some | (live[group] > slot)
            pl.when(some)(add_slot)
        else:
            blank[...] = jnp.zeros(block, jnp.float32)
            for group in range(n_group):
                pl.when(live[group] < cap)(lambda group=group: erase(group).start())
            tokens[0, 0, :, cap - 1] = jnp.zeros((n_group,) + values.shape[4:], jnp.bfloat16)
            lax.fori_loop(0, n_group // SOURCES, run, 0)
            copy = pltpu.make_async_copy(tokens, result, sems.at[n_sem])
            copy.start()
            for group in range(n_group):
                place(group).wait()
                pl.when(live[group] < cap)(lambda group=group: erase(group).wait())
            copy.wait()

    vmem, any_space = pl.BlockSpec(memory_space=pltpu.VMEM), pl.BlockSpec(memory_space=pl.ANY)
    in_vmem = [pltpu.with_memory_space_constraint(x, pltpu.VMEM) for x in sources]
    return pl.pallas_call(
        kernel,
        out_shape=(
            jax.ShapeDtypeStruct(values.shape, jnp.bfloat16),
            jax.ShapeDtypeStruct((1, 1, n_group, cap) + block, jnp.float32),
        ),
        in_specs=[pl.BlockSpec(memory_space=pltpu.SMEM)]
        + [vmem] * (len(sources) + len(small) + 1)
        + [any_space] * len(kept),
        out_specs=(any_space, any_space),
        scratch_shapes=[
            pltpu.VMEM((n_group,) + block, jnp.float32),
            pltpu.SemaphoreType.DMA((2 * n_group + 1,)),
        ]
        + [pltpu.VMEM(shape, jnp.float32) for shape in scratch]
        + [pltpu.VMEM(block, jnp.float32), pltpu.VMEM(values.shape, jnp.bfloat16)],
        input_output_aliases={len(sources) + len(small) + 2 + n: n for n in range(len(kept))},
        compiler_params=pltpu.CompilerParams(vmem_limit_bytes=32 * 1024 * 1024),
    )(live, *in_vmem, *small, gain, *kept)


def exchange(cells):
    return lax.all_to_all(cells, ("group", "sub"), split_axis=0, concat_axis=0, tiled=True)


def with_spare(placed, states, small, gain, n_group):
    cells, live = pack(placed, states, n_group, True)
    heads, key_size, value_size = states.shape[1:]
    square = (key_size, value_size)
    arrived = exchange(cells)
    spare = arrived[:, heads]
    swap = [(n, n ^ 1) for n in range(SUBGROUPS)]
    other = lax.ppermute(spare, "sub", swap)
    by_source = arrived.reshape((n_group, SUBGROUPS, heads + 1) + square)
    other = other.reshape((n_group, SUBGROUPS) + square)
    earlier = decode(
        live, [by_source], lambda s, i, x: [x[s, i, a] for a in range(heads)], 0, small, gain
    )

    def load(s, i, x, y):
        core = lax.axis_index("sub") % CORES
        return [jnp.where(core == a, x[s, i, heads], y[s, i]) for a in range(heads)]

    return decode(live, [by_source, other], load, 1, small, gain, earlier)


def without_spare(placed, states, small, gain, n_group):
    cells, live = pack(placed, states, n_group, False)
    heads, key_size, value_size = states.shape[1:]
    square = (key_size, value_size)
    arrived = exchange(cells).reshape((n_group, SUBGROUPS, SLOT_CAP, heads) + square)
    earlier = None
    for slot in range(SLOT_CAP):
        earlier = decode(
            live,
            [arrived],
            lambda s, i, x, slot=slot: [x[s, i, slot, a] for a in range(heads)],
            slot,
            small,
            gain,
            earlier,
        )
    return earlier


def local(states, placement, queries, key_vectors, value_vectors, gate_inputs, strength, decay, gain):
    n_group = lax.axis_size("group")
    placed = placement.reshape(placement.shape[0])
    fits = cells_fit(placed, n_group * SUBGROUPS, states.shape[0])
    small = (queries, key_vectors, value_vectors, gate_inputs, strength, decay)
    gain = gain.reshape(1, gain.shape[0])
    return lax.switch(
        fits[0],
        [lambda *x: without_spare(*x, n_group), lambda *x: with_spare(*x, n_group)],
        placed,
        states,
        small,
        gain,
    )


def solution(mesh):
    n_group, n_head = mesh.devices.shape
    quads = Mesh(
        mesh.devices.reshape(n_group, n_head // SUBGROUPS, SUBGROUPS), ("group", "block", "sub")
    )
    spread = P("group", ("block", "sub"))
    return jax.shard_map(
        local,
        mesh=quads,
        in_specs=(spread, P(), spread, spread, spread, spread, spread, spread, P()),
        out_specs=(spread, spread),
        check_vma=False,
    )
```

profile of v0, /device:TPU:0, one launch (start us, length us, event | category | flops | bytes accessed | tf_op | source)
XLA Modules:
  0.0 102.1 jit_solution(5451002355512957140)
XLA Ops:
  0.6 1.5 %shard_map.124 = s32[1]{0:T(128)} custom-call(s32[2,128]{1,0:T(2,128)} %bitcast.20), custom_call_target="tpu_custom_call" | custom-call | tf_op jit(solution)/shard_map/pallas_call | solution.py:33
  2.7 99.4 %conditional.1 = ((bf16[1,1,8,2,8,1024]{5,4,3,2,1,0:T(8,128)(2,1)}, f32[1,1,8,2,8,128,128]{6,5,4,3,2,1,0:T(8,128)})) conditional(s32[]{:T(128)} %bitcast.9, (s32[256,1]{0,1:T(1,128)}, f32[32,2,128,128]{3,2,1,0:T(8,128)}, bf16[1,1,8,2,8,512]{5,4,3,2,1,0:T(8,128)(2,1)}, bf16[1,1,8,2,8,512]{5,4,3,2,1,0:T(8,128)(2,1)}, ...), branch_computations={%region_0.0_spmd, %region_1.0_spmd} | conditional | bytes 28346612 | solution.py:425
  2.8 3.9 %branch_1_fun.3 = (f32[32,3,128,128]{3,2,1,0:T(8,128)S(1)}, s32[8]{0:T(128)S(1)}) custom-call(s32[256]{0:T(256)} %bitcast.22, f32[32,2,128,128]{3,2,1,0:T(8,128)} %get-tuple-element.89.refs_1_), custom_call_target="tpu_custom_call" | custom-call | tf_op jit(solution)/shard_map/cond/branch_1_fun/pallas_call | solution.py:96
  6.7 0.0 copy-start.1
  6.7 0.0 copy-start.3
  6.7 0.0 copy-start.5
  6.7 0.0 copy-start.7
  6.7 0.0 copy-start.9
  6.7 0.0 copy-start.11
  6.8 0.0 copy-start.13
  6.8 82.7 %all_to_all.9 = f32[32,3,128,128]{3,2,1,0:T(8,128)S(1)} all-to-all(f32[32,3,128,128]{3,2,1,0:T(8,128)S(1)} %get-tuple-element.52), channel_id=1, replica_groups=mesh['group'=8,'block'=4,'sub'=4] {'group','sub'}, dimensions={0} | all-to-all | bytes 12582912 | tf_op jit(solution)/shard_map/cond/branch_1_fun/all_to_all | solution.py:376
  89.5 0.2 slice_bitcast_fusion
  89.7 1.3 %collective-permute-start = (f32[32,128,128]{2,1,0:T(8,128)S(1)}, f32[32,128,128]{2,1,0:T(8,128)S(1)}, u32[]{:S(2)}, u32[]{:S(2)}) collective-permute-start(f32[32,128,128]{2,1,0:T(8,128)S(1)} %slice_bitcast_fusion), channel_id=1, source_target_pairs={{0,1},{1,0},{2,3},{3,2},{4,5},{5,4},{6,7},{7,6},{8,9},{9,8},{10,11... | collective-permute-start | bytes 6291464 | tf_op jit(solution)/shard_map/cond/branch_1_fun/ppermute | solution.py:386
  91.0 0.0 copy-done.1
  91.0 0.0 copy-done.3
  91.0 0.0 copy-done.5
  91.0 0.0 copy-done.7
  91.0 0.0 copy-done.9
  91.0 0.0 copy-done.11
  91.0 0.0 copy-done.13
  91.0 4.9 %branch_1_fun.4 = (bf16[1,1,8,2,8,1024]{5,4,3,2,1,0:T(8,128)(2,1)}, f32[1,1,8,2,8,128,128]{6,5,4,3,2,1,0:T(8,128)}) custom-call(s32[8]{0:T(128)S(1)} %get-tuple-element.51.live, f32[8,4,3,128,128]{4,3,2,1,0:T(8,128)S(1)} %bitcast.13, bf16[1,1,8,2,8,512]{5,4,3,2,1,0:T(8,128)(2,1)S(1)} %copy-done.5, bf16[1,1,8,2,8,512]{5,4,3,2,1,0:T(8,128)(2,1)S(1)} %copy-done.7, ...), custom_call_target="tpu_custom_call" | custom-call | tf_op jit(solution)/shard_map/cond/branch_1_fun/pallas_call | solution.py:354
  96.0 0.0 collective-permute-done
  96.0 6.2 %branch_1_fun.5 = (bf16[1,1,8,2,8,1024]{5,4,3,2,1,0:T(8,128)(2,1)}, f32[1,1,8,2,8,128,128]{6,5,4,3,2,1,0:T(8,128)}) custom-call(s32[8]{0:T(128)S(1)} %get-tuple-element.51.live, f32[8,4,3,128,128]{4,3,2,1,0:T(8,128)S(1)} %bitcast.14, f32[8,4,128,128]{3,2,1,0:T(8,128)S(1)} %bitcast.15, ...), custom_call_target="tpu_custom_call", output_to_operand_aliasing={{0}: (10, {}), {1}: (11, {})} | custom-call | tf_op jit(solution)/shard_map/cond/branch_1_fun/pallas_call | solution.py:354
Async XLA Ops:
  6.7 84.3 %copy-start.1 = (bf16[1,1,8,2,8,1024]{5,4,3,2,1,0:T(8,128)(2,1)S(1)}, bf16[1,1,8,2,8,1024]{5,4,3,2,1,0:T(8,128)(2,1)}, u32[]{:S(2)}) copy-start(bf16[1,1,8,2,8,1024]{5,4,3,2,1,0:T(8,128)(2,1)} %get-tuple-element.95.refs_3_.refs_4_) | copy-start | bytes 786436 | tf_op jit(solution)/shard_map/cond
  6.7 84.3 %copy-start.3 = (bf16[1,1,8,2,8,1024]{5,4,3,2,1,0:T(8,128)(2,1)S(1)}, bf16[1,1,8,2,8,1024]{5,4,3,2,1,0:T(8,128)(2,1)}, u32[]{:S(2)}) copy-start(bf16[1,1,8,2,8,1024]{5,4,3,2,1,0:T(8,128)(2,1)} %get-tuple-element.97.refs_4_.refs_5_) | copy-start | bytes 786436 | tf_op jit(solution)/shard_map/cond
  6.7 84.3 %copy-start.5 = (bf16[1,1,8,2,8,512]{5,4,3,2,1,0:T(8,128)(2,1)S(1)}, bf16[1,1,8,2,8,512]{5,4,3,2,1,0:T(8,128)(2,1)}, u32[]{:S(2)}) copy-start(bf16[1,1,8,2,8,512]{5,4,3,2,1,0:T(8,128)(2,1)} %get-tuple-element.91.refs_1_.refs_2_) | copy-start | bytes 393220 | tf_op jit(solution)/shard_map/cond
  6.7 84.3 %copy-start.7 = (bf16[1,1,8,2,8,512]{5,4,3,2,1,0:T(8,128)(2,1)S(1)}, bf16[1,1,8,2,8,512]{5,4,3,2,1,0:T(8,128)(2,1)}, u32[]{:S(2)}) copy-start(bf16[1,1,8,2,8,512]{5,4,3,2,1,0:T(8,128)(2,1)} %get-tuple-element.93.refs_2_.refs_3_) | copy-start | bytes 393220 | tf_op jit(solution)/shard_map/cond
  6.7 84.3 %copy-start.9 = (f32[1,1,8,2,8,8]{5,4,3,2,1,0:T(8,128)S(1)}, f32[1,1,8,2,8,8]{5,4,3,2,1,0:T(8,128)}, u32[]{:S(2)}) copy-start(f32[1,1,8,2,8,8]{5,4,3,2,1,0:T(8,128)} %get-tuple-element.99.refs_5_.refs_6_) | copy-start | bytes 12292 | tf_op jit(solution)/shard_map/cond
  6.7 84.3 %copy-start.11 = (f32[1,1,8,2,8,8]{5,4,3,2,1,0:T(8,128)S(1)}, f32[1,1,8,2,8,8]{5,4,3,2,1,0:T(8,128)}, u32[]{:S(2)}) copy-start(f32[1,1,8,2,8,8]{5,4,3,2,1,0:T(8,128)} %get-tuple-element.101.refs_6_.refs_7_) | copy-start | bytes 12292 | tf_op jit(solution)/shard_map/cond
  6.8 84.3 %copy-start.13 = (f32[128]{0:T(128)S(1)}, f32[128]{0:T(128)}, u32[]{:S(2)}) copy-start(f32[128]{0:T(128)} %get-tuple-element.105) | copy-start | bytes 1540 | tf_op jit(solution)/shard_map/cond
  89.7 6.3 %collective-permute-start = (f32[32,128,128]{2,1,0:T(8,128)S(1)}, f32[32,128,128]{2,1,0:T(8,128)S(1)}, u32[]{:S(2)}, u32[]{:S(2)}) collective-permute-start(f32[32,128,128]{2,1,0:T(8,128)S(1)} %slice_bitcast_fusion), channel_id=1, source_target_pairs={{0,1},{1,0},{2,3},{3,2},{4,5},{5,4},{6,7},{7,6},{8,9},{9,8},{10,11... | collective-permute-start | bytes 6291464 | tf_op jit(solution)/shard_map/cond/branch_1_fun/ppermute | solution.py:386
where the time goes:
time: 101 us; the launch traced here: 102 us
  blocking collectives  82.7 us (82%)
  Pallas kernels  16.5 us (16%)
  starting transfers between devices  1.29 us (1%)
  between operations  1.29 us (1%)
    all_to_all x1, blocking collectives, exchange(): lax.all_to_all(cells, ('group', 'sub'), split_axis=0, concat_axis=0, tile...  82.7 us
    pallas_call x2, Pallas kernels, decode(): pl.pallas_call(kernel, out_shape=(jax.ShapeDtypeStruct(values.shape, jnp....  11.1 us
    pallas_call x1, Pallas kernels, pack(): pl.pallas_call(lambda *refs: pack_kernel(n_group, reqs, spare, *refs), ou...  3.92 us
  transfers between devices with their start and end apart: 1, of which 0 were waited for; matrix products, arithmetic and copies ran while one was open for 0% of the time, Pallas kernels for 5%

commit v1 on v0

--- a/solution.py
+++ b/solution.py
@@ -147,13 +147,13 @@
 
 
 def decode_kernel(
-    load, chosen, slot, first, live, query, key, value, gate, strength, decay, gain, tokens, states,
+    load, chosen, sources, slot, first, live, query, key, value, gate, strength, decay, gain, tokens, states,
     by_key, by_query, values, fades, writes, key_rows, query_rows, kept,
 ):
     size, width = states.shape[2:]
     heads = states.shape[1] // SUBGROUPS
     steps = key.shape[4]
-    units = [(n, i) for n in range(SOURCES) for i in range(SUBGROUPS)]
+    units = [(n, i) for n in range(sources) for i in range(SUBGROUPS)]
     count = len(units)
 
     def keys(i):
@@ -182,9 +182,13 @@
             [ref[a, pl.ds(u, steps, stride=count), :] for a in range(heads)], axis=1
         )
 
+    for u, (n, i) in enumerate(units):
+        for ref, x in ((key_rows, key), (query_rows, query)):
+            part = x[0, 0, first + n, slot, :, keys(i)]
+            ref[pl.ds(u, steps, stride=count), :] = part.astype(jnp.float32)
     wide = widen(
         jnp.concatenate(
-            [x[0, 0, first + n, slot] for x in (decay, strength) for n in range(SOURCES)], axis=0
+            [x[0, 0, first + n, slot] for x in (decay, strength) for n in range(sources)], axis=0
         ),
         width,
     )
@@ -204,11 +208,9 @@
         )
         spread(by_key, u, product[:steps])
         spread(by_query, u, product[steps:])
-        key_rows[pl.ds(u, steps, stride=count), :] = key_f
-        query_rows[pl.ds(u, steps, stride=count), :] = query_f
         spread(values, u, value[0, 0, first + n, slot, :, lanes(i)].astype(jnp.float32))
         spread(fades, u, wide[n * steps : (n + 1) * steps, lanes(i)])
-        spread(writes, u, wide[(SOURCES + n) * steps : (SOURCES + n + 1) * steps, lanes(i)])
+        spread(writes, u, wide[(sources + n) * steps : (sources + n + 1) * steps, lanes(i)])
 
     on_key = [[by_key[a, rows(t)] for a in range(heads)] for t in range(steps)]
     on_query = [[by_query[a, rows(t)] for a in range(heads)] for t in range(steps)]
@@ -260,7 +262,7 @@
         token = gather(by_query, u) * (opened * jax.nn.sigmoid(opened))
         tokens[first + n, :, lanes(i)] = token.astype(tokens.dtype)
 
-    for n in range(SOURCES):
+    for n in range(sources):
 
         @pl.when(live[first + n] <= slot)
         def _(n=n):
@@ -274,17 +276,20 @@
     key_size, value_size = queries.shape[5] // SUBGROUPS, gain.shape[1]
     heads = values.shape[5] // (SUBGROUPS * value_size)
     block = (SUBGROUPS * heads, key_size, value_size)
-    units = SOURCES * SUBGROUPS
+    batch_size = SOURCES * 2 if earlier else SOURCES
+    units = batch_size * SUBGROUPS
     rows = steps * units
     by_step = (heads, rows, value_size)
     scratch = [by_step] * 5 + [(rows, key_size)] * 2 + [(units, heads * value_size)]
-    kept = () if earlier is None else earlier
+    kept = () if earlier is None else (earlier[2], *earlier[:2])
 
     def kernel(live, *refs):
         blocks, refs = refs[: len(sources)], refs[len(sources) :]
         ins, refs = refs[: len(small) + 1], refs[len(small) + 1 :]
         before, refs = refs[: len(kept)], refs[len(kept) :]
-        result, finals, states, sems, *work = refs
+        result, finals, *refs = refs
+        handed, refs = refs[: 0 if kept else 1], refs[0 if kept else 1 :]
+        states, sems, *work = refs
         tokens, blank = work.pop(), work.pop()
         n_sem = 2 * n_group
 
@@ -299,32 +304,30 @@
             )
 
         def run(batch, carry):
-            first = batch * SOURCES
+            first = batch * batch_size
 
             def compute():
                 decode_kernel(
-                    lambda s, i: load(s, i, *blocks), len(sources) > 1, slot, first, live, *ins,
-                    tokens.at[0, 0, :, slot], states, *work,
+                    lambda s, i: load(s, i, *blocks), len(sources) > 1, batch_size, slot, first,
+                    live, *ins, tokens.at[0, 0, :, slot], states, *work,
                 )
 
             if kept:
                 some = live[first] > slot
-                for n in range(1, SOURCES):
+                for n in range(1, batch_size):
                     some = some | (live[first + n] > slot)
                 pl.when(some)(compute)
-                for n in range(SOURCES):
+                for n in range(batch_size):
                     pl.when(live[first + n] > slot)(lambda n=n: place(first + n).start())
             else:
                 compute()
-                for n in range(SOURCES):
+                for n in range(batch_size):
                     place(first + n).start()
             return carry
 
         def add_slot():
-            copy = pltpu.make_async_copy(result, tokens, sems.at[n_sem])
-            copy.start()
-            copy.wait()
-            lax.fori_loop(0, n_group // SOURCES, run, 0)
+            lax.fori_loop(0, n_group // batch_size, run, 0)
+            tokens[0, 0, :, 0] = before[0][...]
             copy = pltpu.make_async_copy(tokens, result, sems.at[n_sem])
             copy.start()
             for group in range(n_group):
@@ -332,6 +335,7 @@
             copy.wait()
 
         if kept:
+            tokens[0, 0, :, slot] = jnp.zeros((n_group,) + values.shape[4:], jnp.bfloat16)
             some = live[0] > slot
             for group in range(1, n_group):
                 some = some | (live[group] > slot)
@@ -341,7 +345,8 @@
             for group in range(n_group):
                 pl.when(live[group] < cap)(lambda group=group: erase(group).start())
             tokens[0, 0, :, cap - 1] = jnp.zeros((n_group,) + values.shape[4:], jnp.bfloat16)
-            lax.fori_loop(0, n_group // SOURCES, run, 0)
+            lax.fori_loop(0, n_group // batch_size, run, 0)
+            handed[0][...] = tokens[0, 0, :, slot]
             copy = pltpu.make_async_copy(tokens, result, sems.at[n_sem])
             copy.start()
             for group in range(n_group):
@@ -356,18 +361,21 @@
         out_shape=(
             jax.ShapeDtypeStruct(values.shape, jnp.bfloat16),
             jax.ShapeDtypeStruct((1, 1, n_group, cap) + block, jnp.float32),
-        ),
+        )
+        + (() if kept else (jax.ShapeDtypeStruct((n_group,) + values.shape[4:], jnp.bfloat16),)),
         in_specs=[pl.BlockSpec(memory_space=pltpu.SMEM)]
         + [vmem] * (len(sources) + len(small) + 1)
-        + [any_space] * len(kept),
-        out_specs=(any_space, any_space),
+        + [vmem, any_space, any_space][: len(kept)],
+        out_specs=(any_space, any_space) + (() if kept else (vmem,)),
         scratch_shapes=[
             pltpu.VMEM((n_group,) + block, jnp.float32),
             pltpu.SemaphoreType.DMA((2 * n_group + 1,)),
         ]
         + [pltpu.VMEM(shape, jnp.float32) for shape in scratch]
         + [pltpu.VMEM(block, jnp.float32), pltpu.VMEM(values.shape, jnp.bfloat16)],
-        input_output_aliases={len(sources) + len(small) + 2 + n: n for n in range(len(kept))},
+        input_output_aliases={len(sources) + len(small) + 3 + n: n for n in range(2)}
+        if kept
+        else {},
         compiler_params=pltpu.CompilerParams(vmem_limit_bytes=32 * 1024 * 1024),
     )(live, *in_vmem, *small, gain, *kept)
 

time: 101 us -> 103 us (1.020)
  the two profiles are of different devices: /device:TPU:0 before, /device:TPU:1 now
where the time goes in v1:
time: 103 us; the launch traced here: 102 us
  blocking collectives  84.8 us (82%)
  Pallas kernels  15.8 us (15%)
  between operations  1.29 us (1%)
    all_to_all x1, blocking collectives, exchange(): lax.all_to_all(cells, ('group', 'sub'), split_axis=0, concat_axis=0, tile...  84.8 us
    pallas_call x2, Pallas kernels, decode(): pl.pallas_call(kernel, out_shape=(jax.ShapeDtypeStruct(values.shape, jnp....  10.4 us
    pallas_call x1, Pallas kernels, pack(): pl.pallas_call(lambda *refs: pack_kernel(n_group, reqs, spare, *refs), ou...  3.92 us
  transfers between devices with their start and end apart: 1, of which 0 were waited for; matrix products, arithmetic and copies ran while one was open for 0% of the time, Pallas kernels for 5%

profile of v1, /device:TPU:1, one launch (start us, length us, event | category | flops | bytes accessed | tf_op | source)
XLA Modules:
  0.0 102.4 jit_solution(6177869072492290893)
XLA Ops:
  0.6 1.5 %shard_map.124 = s32[1]{0:T(128)} custom-call(s32[2,128]{1,0:T(2,128)} %bitcast.20), custom_call_target="tpu_custom_call" | custom-call | tf_op jit(solution)/shard_map/pallas_call | solution.py:33
  2.7 99.7 %conditional.1 = ((bf16[1,1,8,2,8,1024]{5,4,3,2,1,0:T(8,128)(2,1)}, f32[1,1,8,2,8,128,128]{6,5,4,3,2,1,0:T(8,128)})) conditional(s32[]{:T(128)} %bitcast.9, (s32[256,1]{0,1:T(1,128)}, f32[32,2,128,128]{3,2,1,0:T(8,128)}, bf16[1,1,8,2,8,512]{5,4,3,2,1,0:T(8,128)(2,1)}, bf16[1,1,8,2,8,512]{5,4,3,2,1,0:T(8,128)(2,1)}, ...), branch_computations={%region_0.0_spmd, %region_1.0_spmd} | conditional | bytes 28346612 | solution.py:433
  2.8 3.9 %branch_1_fun.3 = (f32[32,3,128,128]{3,2,1,0:T(8,128)S(1)}, s32[8]{0:T(128)S(1)}) custom-call(s32[256]{0:T(256)} %bitcast.22, f32[32,2,128,128]{3,2,1,0:T(8,128)} %get-tuple-element.91.refs_1_), custom_call_target="tpu_custom_call" | custom-call | tf_op jit(solution)/shard_map/cond/branch_1_fun/pallas_call | solution.py:96
  6.7 0.0 copy-start.1
  6.7 0.0 copy-start.3
  6.7 0.0 copy-start.5
  6.7 0.0 copy-start.7
  6.7 0.0 copy-start.9
  6.7 0.0 copy-start.11
  6.8 0.0 copy-start.13
  6.8 84.8 %all_to_all.9 = f32[32,3,128,128]{3,2,1,0:T(8,128)S(1)} all-to-all(f32[32,3,128,128]{3,2,1,0:T(8,128)S(1)} %get-tuple-element.53), channel_id=1, replica_groups=mesh['group'=8,'block'=4,'sub'=4] {'group','sub'}, dimensions={0} | all-to-all | bytes 12582912 | tf_op jit(solution)/shard_map/cond/branch_1_fun/all_to_all | solution.py:384
  91.6 0.2 slice_bitcast_fusion
  91.8 0.1 collective-permute-start
  91.9 0.0 copy-done.1
  91.9 0.0 copy-done.3
  91.9 0.0 copy-done.5
  91.9 0.0 copy-done.7
  91.9 0.0 copy-done.9
  91.9 0.0 copy-done.11
  92.0 0.0 copy-done.13
  92.0 5.0 %branch_1_fun.4 = (bf16[1,1,8,2,8,1024]{5,4,3,2,1,0:T(8,128)(2,1)}, f32[1,1,8,2,8,128,128]{6,5,4,3,2,1,0:T(8,128)}, bf16[8,8,1024]{2,1,0:T(8,128)(2,1)S(1)}) custom-call(s32[8]{0:T(128)S(1)} %get-tuple-element.52.live, f32[8,4,3,128,128]{4,3,2,1,0:T(8,128)S(1)} %bitcast.13, bf16[1,1,8,2,8,512]{5,4,3,2,1,0:T(8,128)(2,1)S(1)} %copy-done.5, ...), custom_call_target="tpu_custom_call" | custom-call | tf_op jit(solution)/shard_map/cond/branch_1_fun/pallas_call | solution.py:359
  97.0 0.0 collective-permute-done
  97.0 5.4 %branch_1_fun.5 = (bf16[1,1,8,2,8,1024]{5,4,3,2,1,0:T(8,128)(2,1)}, f32[1,1,8,2,8,128,128]{6,5,4,3,2,1,0:T(8,128)}) custom-call(s32[8]{0:T(128)S(1)} %get-tuple-element.52.live, f32[8,4,3,128,128]{4,3,2,1,0:T(8,128)S(1)} %bitcast.14, f32[8,4,128,128]{3,2,1,0:T(8,128)S(1)} %bitcast.15, ...), custom_call_target="tpu_custom_call", output_to_operand_aliasing={{0}: (11, {}), {1}: (12, {})} | custom-call | tf_op jit(solution)/shard_map/cond/branch_1_fun/pallas_call | solution.py:359
Async XLA Ops:
  6.7 85.2 %copy-start.1 = (bf16[1,1,8,2,8,1024]{5,4,3,2,1,0:T(8,128)(2,1)S(1)}, bf16[1,1,8,2,8,1024]{5,4,3,2,1,0:T(8,128)(2,1)}, u32[]{:S(2)}) copy-start(bf16[1,1,8,2,8,1024]{5,4,3,2,1,0:T(8,128)(2,1)} %get-tuple-element.97.refs_3_.refs_4_) | copy-start | bytes 786436 | tf_op jit(solution)/shard_map/cond
  6.7 85.2 %copy-start.3 = (bf16[1,1,8,2,8,1024]{5,4,3,2,1,0:T(8,128)(2,1)S(1)}, bf16[1,1,8,2,8,1024]{5,4,3,2,1,0:T(8,128)(2,1)}, u32[]{:S(2)}) copy-start(bf16[1,1,8,2,8,1024]{5,4,3,2,1,0:T(8,128)(2,1)} %get-tuple-element.99.refs_4_.refs_5_) | copy-start | bytes 786436 | tf_op jit(solution)/shard_map/cond
  6.7 85.2 %copy-start.5 = (bf16[1,1,8,2,8,512]{5,4,3,2,1,0:T(8,128)(2,1)S(1)}, bf16[1,1,8,2,8,512]{5,4,3,2,1,0:T(8,128)(2,1)}, u32[]{:S(2)}) copy-start(bf16[1,1,8,2,8,512]{5,4,3,2,1,0:T(8,128)(2,1)} %get-tuple-element.93.refs_1_.refs_2_) | copy-start | bytes 393220 | tf_op jit(solution)/shard_map/cond
  6.7 85.2 %copy-start.7 = (bf16[1,1,8,2,8,512]{5,4,3,2,1,0:T(8,128)(2,1)S(1)}, bf16[1,1,8,2,8,512]{5,4,3,2,1,0:T(8,128)(2,1)}, u32[]{:S(2)}) copy-start(bf16[1,1,8,2,8,512]{5,4,3,2,1,0:T(8,128)(2,1)} %get-tuple-element.95.refs_2_.refs_3_) | copy-start | bytes 393220 | tf_op jit(solution)/shard_map/cond
  6.7 85.2 %copy-start.9 = (f32[1,1,8,2,8,8]{5,4,3,2,1,0:T(8,128)S(1)}, f32[1,1,8,2,8,8]{5,4,3,2,1,0:T(8,128)}, u32[]{:S(2)}) copy-start(f32[1,1,8,2,8,8]{5,4,3,2,1,0:T(8,128)} %get-tuple-element.101.refs_5_.refs_6_) | copy-start | bytes 12292 | tf_op jit(solution)/shard_map/cond
  6.7 85.2 %copy-start.11 = (f32[1,1,8,2,8,8]{5,4,3,2,1,0:T(8,128)S(1)}, f32[1,1,8,2,8,8]{5,4,3,2,1,0:T(8,128)}, u32[]{:S(2)}) copy-start(f32[1,1,8,2,8,8]{5,4,3,2,1,0:T(8,128)} %get-tuple-element.103.refs_6_.refs_7_) | copy-start | bytes 12292 | tf_op jit(solution)/shard_map/cond
  6.8 85.2 %copy-start.13 = (f32[128]{0:T(128)S(1)}, f32[128]{0:T(128)}, u32[]{:S(2)}) copy-start(f32[128]{0:T(128)} %get-tuple-element.107) | copy-start | bytes 1540 | tf_op jit(solution)/shard_map/cond
  91.8 5.2 %collective-permute-start = (f32[32,128,128]{2,1,0:T(8,128)S(1)}, f32[32,128,128]{2,1,0:T(8,128)S(1)}, u32[]{:S(2)}, u32[]{:S(2)}) collective-permute-start(f32[32,128,128]{2,1,0:T(8,128)S(1)} %slice_bitcast_fusion), channel_id=1, source_target_pairs={{0,1},{1,0},{2,3},{3,2},{4,5},{5,4},{6,7},{7,6},{8,9},{9,8},{10,11... | collective-permute-start | bytes 6291464 | tf_op jit(solution)/shard_map/cond/branch_1_fun/ppermute | solution.py:394
